TPU v7x, 512 devices: a whole 4x4x16 slice. The times are simulated.
512 devices in a mesh: leaf: 64 (over y, z), cols: 8 (over x, core).
Axes of the slice: x: 4, y: 4, z: 16, core: 2. Of those that a mesh axis runs over, the one named last changes fastest.
Arguments:
- points: float32 [3, 131072], P(None, 'leaf'), may hold values from 0 to 1
- samples: float32 [256, 131072], P('cols', 'leaf'), may hold values from -6 to 6
- sketch: float32 [32, 256], P(None, 'cols'), may hold values from -0.375 to 0.375
- far_requests: int32 [64, 64, 8], P('leaf'), may hold values from 0 to 31, as said below
- far_slots: int32 [2048, 16], P('leaf'), may hold values from 0 to 511, as said below
- far_count: int32 [2048], P('leaf'), may hold values from 1 to 16, as said below
- near_mask: int32 [2048, 3], P('leaf'), may hold values 0 or 1
Outputs:
- far_sample: float32 [256, 131072], P('cols', 'leaf')
- near_sample: float32 [256, 131072], P('cols', 'leaf')
- leaf_basis: float32 [32, 131072], P(None, 'leaf')
- branch_samples: float32 [2048, 256], P('leaf', 'cols')
- top_transfer: float32 [63, 64, 32], replicated
- root_sample: float32 [32, 256], P(None, 'cols')
Inputs may be any that keep to these rules, and one draw needn't show every extreme that they name: far_requests[e, d, c] is a leaf counted on device d of leaf (0 for its first); the 8 entries of each [e, d] are distinct. far_slots[i, f] names slot far_slots[i, f] mod 8 of the clusters fetched from device far_slots[i, f] // 8; only entries f < far_count[i] are used; among the 512 entries (used or not) of the leaves of one device, no device is named by more than 8 entries, and some device by exactly 8. `far_count`: used entries of each leaf's far-field list.
All inputs are finite; a program needn't handle non-finite values. No bound on the sum of `near_mask` on one device may be relied on, other than what follows from the above.
Results may differ from a plain program's by a relative error of at most 0.0003.
Values sent between devices are 32-bit elements; how exact they have to be, the bound alone decides.
A program may use at most 64 MiB of HBM per device.

v0:
```python
import jax
import jax.numpy as jnp
import numpy as np
from jax import lax
from jax.sharding import PartitionSpec as P

LEAF = 64
FAR = 16
NS = 1


length_scale = 0.3
shift_share = 0.05
highest = lax.Precision.HIGHEST


def with_halo(block, sides, width):
    for axis, dim in sides:
        count = lax.axis_size(axis)
        forward = [(i, i + 1) for i in range(count - 1)]
        backward = [(target, source) for source, target in forward]
        low = lax.ppermute(
            lax.slice_in_dim(block, block.shape[dim] - width, None, axis=dim), axis, forward
        )
        high = lax.ppermute(lax.slice_in_dim(block, 0, width, axis=dim), axis, backward)
        block = jnp.concatenate([low, block, high], axis=dim)
    return block


def swapped(array, axis, stride):
    return lax.ppermute(array, axis, [(i, i ^ 1 << stride) for i in range(lax.axis_size(axis))])


def kernel_last(source_coords, target_coords):
    differences = source_coords[:, :, None, :] - target_coords[:, None, :, :]
    return jnp.exp(-jnp.sqrt(jnp.sum(differences * differences, axis=0)) / length_scale)


def factor(sketched):
    gram_matrix = jnp.einsum("nmr,nmq->nrq", sketched, sketched, precision=highest)
    order_size = gram_matrix.shape[-1]
    trace_sum = jnp.trace(gram_matrix, axis1=1, axis2=2)
    shifted = gram_matrix + (shift_share * trace_sum / order_size + 1e-06)[:, None, None] * jnp.eye(
        order_size, dtype=jnp.float32
    )
    lower_factor = jnp.linalg.cholesky(shifted)
    return jax.scipy.linalg.solve_triangular(lower_factor, jnp.swapaxes(sketched, 1, 2), lower=True)


def inner_level(current, sketch):
    stacked = current.reshape(current.shape[0] // 2, 2 * current.shape[1], current.shape[2])
    partial_value = jnp.einsum("nms,rs->nmr", stacked, sketch, precision=highest)
    summed = lax.psum(partial_value, "cols")
    transfer_t = factor(summed)
    return jnp.einsum("nrm,nms->nrs", transfer_t, stacked, precision=highest)


def on_device(points, samples, sketch, far_requests, far_slots, far_count, near_mask):
    samp_dev = samples.shape[0]
    leaves_dev = samples.shape[1] // LEAF
    rank_size = sketch.shape[0]
    coords = points.reshape(3, leaves_dev, LEAF)
    sample_blocks = samples.reshape(samp_dev, leaves_dev, LEAF)
    target_coords = jnp.transpose(coords, (0, 2, 1))
    wanted = far_requests.reshape(far_requests.shape[1], far_requests.shape[2])
    packed_samples = jnp.transpose(sample_blocks, (1, 0, 2)).reshape(leaves_dev, samp_dev * LEAF)
    packed_coords = jnp.transpose(coords, (1, 0, 2)).reshape(leaves_dev, 3 * LEAF)
    start = jnp.zeros((samp_dev, LEAF, leaves_dev), jnp.float32)
    asked_for = lax.all_to_all(wanted, "leaf", split_axis=0, concat_axis=0, tiled=True)
    blocks = packed_samples[asked_for]
    places = packed_coords[asked_for]
    fetched = lax.all_to_all(blocks, "leaf", split_axis=0, concat_axis=0, tiled=True)
    fetched_coords = lax.all_to_all(places, "leaf", split_axis=0, concat_axis=0, tiled=True)
    fetched = fetched.reshape(-1, samp_dev * LEAF)
    fetched_coords = fetched_coords.reshape(-1, 3 * LEAF)

    def far_step(slot_index, accumulated):
        slot_ids = lax.dynamic_index_in_dim(far_slots, slot_index, 1, keepdims=False)
        blocks = jnp.transpose(fetched[slot_ids].reshape(leaves_dev, samp_dev, LEAF), (1, 2, 0))
        source_coords = jnp.transpose(
            fetched_coords[slot_ids].reshape(leaves_dev, 3, LEAF), (1, 2, 0)
        )
        weight = (slot_index < far_count).astype(jnp.float32)
        kernel_vals = kernel_last(source_coords, target_coords) * weight
        return accumulated + jnp.einsum("spl,pql->sql", blocks, kernel_vals, precision=highest)

    far_acc = lax.fori_loop(0, FAR, far_step, start)
    joined = jnp.concatenate([samples, points], axis=0)
    widened = with_halo(joined, (("leaf", 1),), NS * LEAF)
    widened = widened.reshape(samp_dev + 3, leaves_dev + 2 * NS, LEAF)
    near_weights = near_mask.astype(jnp.float32)
    near_acc = start
    for offset in range(2 * NS + 1):
        window = widened[:, offset : offset + leaves_dev, :]
        source_samples = jnp.transpose(window[:samp_dev], (0, 2, 1))
        source_coords = jnp.transpose(window[samp_dev:], (0, 2, 1))
        kernel_vals = kernel_last(source_coords, target_coords) * near_weights[:, offset]
        near_acc = near_acc + jnp.einsum(
            "spl,pql->sql", source_samples, kernel_vals, precision=highest
        )
    far_sample = jnp.transpose(far_acc, (0, 2, 1)).reshape(samp_dev, leaves_dev * LEAF)
    near_sample = jnp.transpose(near_acc, (0, 2, 1)).reshape(samp_dev, leaves_dev * LEAF)
    sample_rows = jnp.transpose(far_acc, (2, 1, 0))
    partial_value = jnp.einsum("lps,rs->lpr", sample_rows, sketch, precision=highest)
    summed = lax.psum(partial_value, "cols")
    basis_t = factor(summed)
    leaf_basis = jnp.transpose(basis_t, (1, 0, 2)).reshape(rank_size, leaves_dev * LEAF)
    current = jnp.einsum("lrp,lps->lrs", basis_t, sample_rows, precision=highest)
    while current.shape[0] > 1:
        current = inner_level(current, sketch)
    branch_samples = current.reshape(rank_size, samp_dev)
    branches = lax.axis_size("leaf")
    tree_depth = branches.bit_length() - 1
    my_index = lax.axis_index("leaf")
    my_next = my_index + 1
    own_transfer = jnp.zeros((2 * rank_size, rank_size), jnp.float32)
    for tree_level in range(tree_depth):
        partner = swapped(current, "leaf", tree_level)
        on_left = (my_index >> tree_level) % 2 == 0
        stacked = jnp.where(
            on_left,
            jnp.concatenate([current, partner], axis=1),
            jnp.concatenate([partner, current], axis=1),
        )
        partial_top = jnp.einsum("nms,rs->nmr", stacked, sketch, precision=highest)
        summed_top = lax.psum(partial_top, "cols")
        transfer_t = factor(summed_top)
        current = jnp.einsum("nrm,nms->nrs", transfer_t, stacked, precision=highest)
        mine = (my_next % 2 ** (tree_level + 1) == 2**tree_level).astype(jnp.float32)
        own_transfer = own_transfer + mine * jnp.swapaxes(transfer_t[0], 0, 1)
    collected, roots = (
        lax.all_gather(own_transfer[None], "leaf", axis=0, tiled=True),
        lax.all_gather(current, "leaf", axis=0, tiled=True),
    )
    device_list = []
    for tree_level in range(tree_depth):
        for node_index in range(branches >> tree_level + 1):
            device_list.append(node_index * 2 ** (tree_level + 1) + 2**tree_level - 1)
    top_transfer = collected[np.array(device_list, dtype=np.int32)]
    root_sample = roots[branches - 1]
    return (far_sample, near_sample, leaf_basis, branch_samples, top_transfer, root_sample)


def solution(mesh):
    return jax.shard_map(
        on_device,
        mesh=mesh,
        in_specs=(
            P(None, "leaf"),
            P("cols", "leaf"),
            P(None, "cols"),
            P("leaf", None, None),
            P("leaf", None),
            P("leaf"),
            P("leaf", None),
        ),
        out_specs=(
            P("cols", "leaf"),
            P("cols", "leaf"),
            P(None, "leaf"),
            P("leaf", "cols"),
            P(),
            P(None, "cols"),
        ),
        check_vma=False,
    )
```

profile of v0, /device:TPU:8, one launch (start us, length us, event | category | flops | bytes accessed | tf_op | source)
XLA Modules:
  0.0 1447.4 jit_solution(18267569821181476500)
XLA Ops:
  8.6 18.9 %all-to-all-start = ((s32[64,1,8]{2,1,0:T(1,128)}), s32[64,1,8]{2,1,0:T(1,128)S(1)}, u32[]{:S(2)}, u32[]{:S(2)}) async-start(s32[64,1,8]{2,1,0:T(1,128)} %bitcast.1), calls=%async_computation | async-start | bytes 65536 | tf_op jit(solution)/shard_map/all_to_all | solution.py:69
  53.1 25.7 %all-to-all-done.1 = f32[64,8,192]{2,1,0:T(8,128)S(1)} async-done(((f32[64,8,192]{2,1,0:T(8,128)}), f32[64,8,192]{2,1,0:T(8,128)S(1)}, u32[]{:S(2)}, u32[]{:S(2)}) %all-to-all-start.1) | async-done | bytes 393248 | tf_op jit(solution)/shard_map/all_to_all | solution.py:73
  94.7 176.1 %all-to-all-done.2 = f32[64,8,2048]{2,1,0:T(8,128)} async-done(((f32[64,8,2048]{2,1,0:T(8,128)}), f32[64,8,2048]{2,1,0:T(8,128)}, u32[]{:S(2)}, u32[]{:S(2)}) %all-to-all-start.2) | async-done | bytes 4194336 | tf_op jit(solution)/shard_map/all_to_all | solution.py:72
  270.9 124.8 %while.14 = (s32[]{:T(128)}, f32[32,64,32]{1,0,2:T(8,128)S(1)}, s32[32,16]{0,1:T(8,128)}, f32[512,192]{1,0:T(8,128)S(1)}, f32[3,64,32]{1,2,0:T(8,128)S(1)}, /*in...) while((s32[]{:T(128)}, f32[32,64,32]{1,0,2:T(8,128)S(1)}, s32[32,16]{0,1:T(8,128)}, ...), condition=%wide.region_2.3_spmd.clone, body=%wide.region_0.2_spmd.clone.sunk | while | flops 51905696 | bytes 4133999 | solution.py:87
  398.1 71.3 %all-reduce.4.cloned.1.call-done = f32[32,64,32]{1,2,0:T(8,128)} async-done(((f32[32,64,32]{1,2,0:T(8,128)}), f32[32,64,32]{1,2,0:T(8,128)}) %all-reduce.4.cloned.1.call-update) | async-done | bytes 262160 | tf_op jit(solution)/shard_map/psum | solution.py:105
  472.5 93.8 %custom-call.46 = f32[32,32,32]{2,1,0:T(8,128)S(1)} custom-call(f32[32,32,32]{2,1,0:T(8,128)S(1)} %fusion.10), custom_call_target="Cholesky" | custom-call | tf_op jit(solution)/shard_map/jit(cholesky)/cholesky | solution.py:46
  567.1 12.5 custom-call.47
  584.4 74.2 %all-reduce.6.cloned.1.call-done = f32[16,64,32]{1,2,0:T(8,128)} async-done(((f32[16,64,32]{1,2,0:T(8,128)}), f32[16,64,32]{1,2,0:T(8,128)}) %all-reduce.6.cloned.1.call-update) | async-done | bytes 131088 | tf_op jit(solution)/shard_map/psum | solution.py:53
  661.3 47.6 %custom-call.48 = f32[16,32,32]{2,1,0:T(8,128)S(1)} custom-call(f32[16,32,32]{2,1,0:T(8,128)} %fusion.18), custom_call_target="Cholesky" | custom-call | tf_op jit(solution)/shard_map/jit(cholesky)/cholesky | solution.py:46
  709.1 39.4 %custom-call.49 = f32[16,1,32,32]{2,3,1,0:T(8,128)S(1)} custom-call(f32[16,1,32,32]{3,2,1,0:T(8,128)S(1)} %select_bitcast_fusion.1), custom_call_target="InvertDiagBlocksLowerTriangular" | custom-call | tf_op jit(solution)/shard_map/jit(_solve_triangular)/vmap()/triangular_solve | solution.py:47
  757.2 68.9 %all-reduce.8.cloned.1.call-done = f32[8,64,32]{1,2,0:T(8,128)} async-done(((f32[8,64,32]{1,2,0:T(8,128)}), f32[8,64,32]{1,2,0:T(8,128)}) %all-reduce.8.cloned.1.call-update) | async-done | bytes 65552 | tf_op jit(solution)/shard_map/psum | solution.py:53
  827.7 23.4 %custom-call.50 = f32[8,32,32]{2,1,0:T(8,128)S(1)} custom-call(f32[8,32,32]{2,1,0:T(8,128)S(1)} %fusion.22), custom_call_target="Cholesky" | custom-call | tf_op jit(solution)/shard_map/jit(cholesky)/cholesky | solution.py:46
  851.4 19.7 %custom-call.51 = f32[8,1,32,32]{2,3,1,0:T(8,128)S(1)} custom-call(f32[8,1,32,32]{3,2,1,0:T(8,128)S(1)} %select_bitcast_fusion.2), custom_call_target="InvertDiagBlocksLowerTriangular" | custom-call | tf_op jit(solution)/shard_map/jit(_solve_triangular)/vmap()/triangular_solve | solution.py:47
  873.3 24.9 %psum.87 = f32[4,64,32]{1,2,0:T(8,128)S(1)} all-reduce(f32[4,64,32]{1,2,0:T(8,128)S(1)} %fusion.75), channel_id=1, replica_groups=mesh['leaf'=64,'cols'=8] {'cols'}, use_global_device_ids=true, to_apply=%region_18.19 | all-reduce | flops 8192 | bytes 65536 | tf_op jit(solution)/shard_map/psum | solution.py:53
  921.3 23.6 %psum.88 = f32[2,64,32]{1,2,0:T(8,128)S(1)} all-reduce(f32[2,64,32]{1,2,0:T(8,128)S(1)} %fusion.73), channel_id=1, replica_groups=mesh['leaf'=64,'cols'=8] {'cols'}, use_global_device_ids=true, to_apply=%region_22.23 | all-reduce | flops 4096 | bytes 32768 | tf_op jit(solution)/shard_map/psum | solution.py:53
  957.0 23.6 %psum.89 = f32[1,64,32]{1,2,0:T(8,128)S(1)} all-reduce(f32[1,64,32]{1,2,0:T(8,128)S(1)} %convolution_bitcast_fusion.7), channel_id=1, replica_groups=mesh['leaf'=64,'cols'=8] {'cols'}, use_global_device_ids=true, to_apply=%region_26.27 | all-reduce | flops 2048 | bytes 16384 | tf_op jit(solution)/shard_map/psum | solution.py:53
  996.2 23.6 %psum.90 = f32[1,64,32]{1,2,0:T(8,128)S(1)} all-reduce(f32[1,64,32]{1,2,0:T(8,128)S(1)} %convolution_bitcast_fusion.6), channel_id=1, replica_groups=mesh['leaf'=64,'cols'=8] {'cols'}, use_global_device_ids=true, to_apply=%region_30.33 | all-reduce | flops 2048 | bytes 16384 | tf_op jit(solution)/shard_map/psum | solution.py:126
  1035.7 23.6 %psum.91 = f32[1,64,32]{1,2,0:T(8,128)S(1)} all-reduce(f32[1,64,32]{1,2,0:T(8,128)S(1)} %convolution_bitcast_fusion.5), channel_id=1, replica_groups=mesh['leaf'=64,'cols'=8] {'cols'}, use_global_device_ids=true, to_apply=%region_32.35 | all-reduce | flops 2048 | bytes 16384 | tf_op jit(solution)/shard_map/psum | solution.py:126
  1077.8 23.6 %psum.92 = f32[1,64,32]{1,2,0:T(8,128)S(1)} all-reduce(f32[1,64,32]{1,2,0:T(8,128)S(1)} %convolution_bitcast_fusion.4), channel_id=1, replica_groups=mesh['leaf'=64,'cols'=8] {'cols'}, use_global_device_ids=true, to_apply=%region_34.37 | all-reduce | flops 2048 | bytes 16384 | tf_op jit(solution)/shard_map/psum | solution.py:126
  1125.5 23.8 %psum.93 = f32[1,64,32]{1,2,0:T(8,128)S(1)} all-reduce(f32[1,64,32]{1,2,0:T(8,128)S(1)} %convolution_bitcast_fusion.3), channel_id=1, replica_groups=mesh['leaf'=64,'cols'=8] {'cols'}, use_global_device_ids=true, to_apply=%region_36.39 | all-reduce | flops 2048 | bytes 16384 | tf_op jit(solution)/shard_map/psum | solution.py:126
  1164.1 23.6 %psum.94 = f32[1,64,32]{1,2,0:T(8,128)S(1)} all-reduce(f32[1,64,32]{1,2,0:T(8,128)S(1)} %convolution_bitcast_fusion.2), channel_id=1, replica_groups=mesh['leaf'=64,'cols'=8] {'cols'}, use_global_device_ids=true, to_apply=%region_38.41 | all-reduce | flops 2048 | bytes 16384 | tf_op jit(solution)/shard_map/psum | solution.py:126
  1207.0 23.6 %psum.95 = f32[1,64,32]{1,2,0:T(8,128)S(1)} all-reduce(f32[1,64,32]{1,2,0:T(8,128)S(1)} %convolution_bitcast_fusion.1), channel_id=1, replica_groups=mesh['leaf'=64,'cols'=8] {'cols'}, use_global_device_ids=true, to_apply=%region_40.43 | all-reduce | flops 2048 | bytes 16384 | tf_op jit(solution)/shard_map/psum | solution.py:126
  1239.3 99.8 %all-gather.1 = f32[2048,32]{1,0:T(8,128)S(1)} all-gather(f32[32,32]{1,0:T(8,128)S(1)} %fusion.91), channel_id=3, replica_groups=mesh['leaf'=64,'cols'=8] {'leaf'}, dimensions={0}, use_global_device_ids=true | all-gather | bytes 266240 | tf_op jit(solution)/shard_map/all_gather | solution.py:133
  1339.7 99.1 %all-gather.2 = f32[64,64,32]{1,2,0:T(8,128)S(1)} all-gather(f32[1,64,32]{1,2,0:T(8,128)S(1)} %add_bitcast_fusion), channel_id=2, replica_groups=mesh['leaf'=64,'cols'=8] {'leaf'}, dimensions={0}, use_global_device_ids=true | all-gather | bytes 532480 | tf_op jit(solution)/shard_map/all_gather | solution.py:132
  (405 shorter events, 342.3 us)
Async XLA Ops:
  7.2 388.5 %copy-start = (f32[32,32]{1,0:T(8,128)S(1)}, f32[32,32]{1,0:T(8,128)}, u32[]{:S(2)}) copy-start(f32[32,32]{1,0:T(8,128)} %param.16) | copy-start | bytes 12292
  8.6 40.2 %copy-start.2 = (f32[32,2048]{1,0:T(8,128)S(1)}, f32[32,2048]{1,0:T(8,128)}, u32[]{:S(2)}) copy-start(f32[32,2048]{1,0:T(8,128)} %param.15) | copy-start | bytes 786436
  8.6 32.3 %all-to-all-start = ((s32[64,1,8]{2,1,0:T(1,128)}), s32[64,1,8]{2,1,0:T(1,128)S(1)}, u32[]{:S(2)}, u32[]{:S(2)}) async-start(s32[64,1,8]{2,1,0:T(1,128)} %bitcast.1), calls=%async_computation | async-start | bytes 65536 | tf_op jit(solution)/shard_map/all_to_all | solution.py:69
  43.2 35.6 %all-to-all-start.1 = ((f32[64,8,192]{2,1,0:T(8,128)}), f32[64,8,192]{2,1,0:T(8,128)S(1)}, u32[]{:S(2)}, u32[]{:S(2)}) async-start(f32[64,8,192]{2,1,0:T(8,128)} %bitcast.3), calls=%async_computation.1 | async-start | bytes 1048576 | tf_op jit(solution)/shard_map/all_to_all | solution.py:73
  78.8 7.8 copy-start.3
  78.8 15.8 %copy-start.4 = (s32[32,3]{0,1:T(4,128)S(1)}, s32[32,3]{0,1:T(4,128)}, u32[]{:S(2)}) copy-start(s32[32,3]{0,1:T(4,128)} %param.20) | copy-start | bytes 1156
  78.8 192.0 %copy-start.6 = (s32[32]{0:T(128)S(1)}, s32[32]{0:T(128)}, u32[]{:S(2)}) copy-start(s32[32]{0:T(128)} %param.19) | copy-start | bytes 388
  78.8 192.0 %all-to-all-start.2 = ((f32[64,8,2048]{2,1,0:T(8,128)}), f32[64,8,2048]{2,1,0:T(8,128)}, u32[]{:S(2)}, u32[]{:S(2)}) async-start(f32[64,8,2048]{2,1,0:T(8,128)} %bitcast.353), calls=%async_computation.2 | async-start | bytes 8388608 | tf_op jit(solution)/shard_map/all_to_all | solution.py:72
  86.5 382.9 %all-reduce.4.cloned.1.call-start = ((), (), s32[]{:S(2)}) async-start(), calls=%async_computation.3 | async-start | bytes 1048576 | tf_op jit(solution)/shard_map/psum | solution.py:105
  86.7 310.9 %collective-permute-start = (f32[35,64]{1,0:T(8,128)S(1)}, f32[35,64]{1,0:T(8,128)S(1)}, u32[]{:S(2)}, u32[]{:S(2)}) collective-permute-start(f32[35,64]{1,0:T(8,128)S(1)} %get-tuple-element.219), channel_id=1, source_target_pairs={{0,8},{8,16},{16,24},{24,32},{32,40},{40,48},{48,56},{56,64},{64,7... | collective-permute-start | bytes 26888 | tf_op jit(solution)/shard_map/ppermute | solution.py:22
  90.1 307.6 %collective-permute-start.1 = (f32[35,64]{1,0:T(8,128)S(1)}, f32[35,64]{1,0:T(8,128)S(1)}, u32[]{:S(2)}, u32[]{:S(2)}) collective-permute-start(f32[35,64]{1,0:T(8,128)S(1)} %get-tuple-element.218), channel_id=1, source_target_pairs={{8,0},{16,8},{24,16},{32,24},{40,32},{48,40},{56,48},{64,56},{72,6... | collective-permute-start | bytes 26888 | tf_op jit(solution)/shard_map/ppermute | solution.py:25
  270.9 126.4 %copy-start.5 = (s32[63]{0:T(128)S(1)}, s32[63]{0:T(128)}, u32[]{:S(2)}) copy-start(s32[63]{0:T(128)} %constant.506) | copy-start | bytes 760
  397.1 261.5 %all-reduce.6.cloned.1.call-start = ((), (), s32[]{:S(2)}) async-start(), calls=%async_computation.4 | async-start | bytes 524288 | tf_op jit(solution)/shard_map/psum | solution.py:53
  472.1 108.0 %copy-start.1 = (f32[32,64,32]{1,2,0:T(8,128)S(1)}, f32[32,64,32]{1,2,0:T(8,128)}, u32[]{:S(2)}) copy-start(f32[32,64,32]{1,2,0:T(8,128)} %all-reduce.4.cloned.1.call-done) | copy-start | bytes 786436
  584.0 242.1 %all-reduce.8.cloned.1.call-start = ((), (), s32[]{:S(2)}) async-start(), calls=%async_computation.5 | async-start | bytes 262144 | tf_op jit(solution)/shard_map/psum | solution.py:53
  989.2 6.8 collective-permute-start.2
  1028.4 7.1 collective-permute-start.3
  1067.9 9.6 collective-permute-start.4
  1110.0 15.3 %collective-permute-start.5 = (f32[1,32,32]{1,2,0:T(8,128)S(1)}, f32[1,32,32]{1,2,0:T(8,128)S(1)}, u32[]{:S(2)}, u32[]{:S(2)}) collective-permute-start(f32[1,32,32]{1,2,0:T(8,128)S(1)} %bitcast.376), channel_id=1, source_target_pairs={{0,64},{8,72},{16,80},{24,88},{32,96},{40,104},{48,112},{56,120},{... | collective-permute-start | bytes 12296 | tf_op jit(solution)/shard_map/ppermute | solution.py:31
  1158.0 5.9 collective-permute-start.6
  1196.3 10.5 collective-permute-start.7
Sparse Core Ops, SparseCore 0:
  397.2 72.1 all-reduce.3
  584.1 74.4 all-reduce.5
  752.3 73.7 all-reduce.7
where the time goes:
time: 1460 us; the launch traced here: 1450 us
  waiting for transfers between devices  430 us (29%)
  blocking collectives  413 us (28%)
  other arithmetic  364 us (25%)
  local copies, waits for them, and re-layouts  83.1 us (6%)
  starting transfers between devices  73.9 us (5%)
  matrix products  62.9 us (4%)
  between operations  19.8 us (1%)
    another operation x37, other arithmetic, factor(): lower_factor = jnp.linalg.cholesky(shifted)  208 us
    all_to_all x1, waiting for transfers between devices, on_device(): lax.all_to_all(blocks, 'leaf', split_axis=0, concat_axis=0, tiled=True)  176 us
    psum x2, waiting for transfers between devices, inner_level(): summed = lax.psum(partial_value, 'cols')  143 us
    psum x6, blocking collectives, on_device(): summed_top = lax.psum(partial_top, 'cols')  142 us
    another operation x25, other arithmetic, factor(): jax.scipy.linalg.solve_triangular(lower_factor, jnp.swapaxes(sketched, 1,...  108 us
    all_gather x1, blocking collectives, on_device(): lax.all_gather(current, 'leaf', axis=0, tiled=True)  99.8 us
    all_gather x1, blocking collectives, on_device(): lax.all_gather(own_transfer[None], 'leaf', axis=0, tiled=True)  99.1 us
    psum x3, blocking collectives, inner_level(): summed = lax.psum(partial_value, 'cols')  72 us
  transfers between devices with their start and end apart: 14, of which 7 were waited for; matrix products, arithmetic and copies ran while one was open for 11% of the time, Pallas kernels for 0%

commit v1 on v0

v1 whole, which is shorter than its diff:
```python
import functools

import jax
import jax.numpy as jnp
from jax import lax
from jax.experimental import pallas as pl
from jax.experimental.pallas import tpu as pltpu
from jax.sharding import PartitionSpec as P

LEAF = 64
FAR = 16
CAP = 8
RANK = 32
NEAR = 3
ROWS_Y = 4
CELL = 16
HALF = 16
SUB = HALF * CELL + HALF * 2
MSG = CAP * CELL + CAP * 2
NODE = 24

length_scale = 0.3
shift_share = 0.05
highest = lax.Precision.HIGHEST
MESH = pl.DeviceIdType.MESH
VMEM = pltpu.VMEM
whole = pl.BlockSpec(memory_space=pltpu.VMEM)
scalars = pl.BlockSpec(memory_space=pltpu.SMEM)
MIB = 1 << 20


def lanes(shape):
    return lax.broadcasted_iota(jnp.int32, shape, len(shape) - 1)


def swap_halves(tile):
    return pltpu.roll(tile, 64, 1)


def dot_nt(a, b, precision=highest):
    return lax.dot_general(
        a, b, (((1,), (1,)), ((), ())), precision=precision, preferred_element_type=jnp.float32
    )


def dot_nn(a, b, precision=highest):
    return lax.dot_general(
        a, b, (((1,), (0,)), ((), ())), precision=precision, preferred_element_type=jnp.float32
    )


def greet(axis, peers):
    barrier = pltpu.get_barrier_semaphore()
    for peer in peers:
        pl.semaphore_signal(barrier, inc=1, device_id={axis: peer}, device_id_type=MESH)
    pl.semaphore_wait(barrier, len(peers))


def fetch_body(
    n_leaf, samples, coords, own_requests, sent_requests, recv, local, halo, *scratch
):
    n_y = ROWS_Y
    n_z = n_leaf // n_y
    chunks = (local,) + scratch[: n_z - 1]
    stage, edge, asked_v, asked, ring_send, ring_recv, y_send, y_recv, q_send, q_recv, q_local, e_send, e_recv = scratch[n_z - 1 :]
    me = lax.axis_index("leaf")
    y, z = me // n_z, me % n_z
    up = y * n_z + (z + 1) % n_z
    down = y * n_z + (z + n_z - 1) % n_z
    above, below = (me + 1) % n_leaf, (me + n_leaf - 1) % n_leaf
    across = [None] + [((y + k) % n_y) * n_z + z for k in range(1, n_y)]
    greet("leaf", [up, down, above, below] + across[1:])

    def remote(src, dst, send, recv_sem, peer):
        return pltpu.make_async_remote_copy(
            src_ref=src, dst_ref=dst, send_sem=send, recv_sem=recv_sem,
            device_id={"leaf": peer}, device_id_type=MESH,
        )

    sent = []
    asks = []
    for k in range(1, n_y):
        copy = remote(
            sent_requests.at[(y + k) % n_y], asked_v.at[n_y - k - 1], q_send.at[k - 1], q_recv.at[n_y - k - 1], across[k]
        )
        copy.start()
        asks.append(copy)
    sent += asks

    low = lanes((CELL, 2 * LEAF)) < LEAF
    for j in range(HALF):
        top = samples[0:CELL, 2 * LEAF * j : 2 * LEAF * (j + 1)]
        bottom = samples[CELL : 2 * CELL, 2 * LEAF * j : 2 * LEAF * (j + 1)]
        base = (2 * j // HALF) * SUB + (2 * j % HALF) * CELL
        local[base : base + CELL, :] = jnp.where(low, top, swap_halves(bottom))
        local[base + CELL : base + 2 * CELL, :] = jnp.where(low, swap_halves(top), bottom)
    for h in range(2):
        local[h * SUB + HALF * CELL : (h + 1) * SUB, :] = coords[2 * HALF * h : 2 * HALF * (h + 1), :]

    hops = {(0, 0): n_z // 2, (0, 1): n_z // 2 - 1, (1, 0): n_z // 2 - 1, (1, 1): n_z // 2}

    def ring(way, part, step):
        here, there = (step, step + 1) if way == 0 else ((n_z - step) % n_z, n_z - step - 1)
        rows = pl.ds(part * SUB, SUB)
        return remote(
            chunks[here].at[rows], chunks[there].at[rows], ring_send.at[way, part, step],
            ring_recv.at[way, part, step], up if way == 0 else down,
        )

    def forward(way, part, step):
        if step < hops[way, part]:
            copy = ring(way, part, step)
            copy.start()
            sent.append(copy)

    order = ((0, 0), (1, 1), (0, 1), (1, 0))
    for way, part in order:
        forward(way, part, 0)

    for side, cluster in ((0, 0), (1, 2 * HALF - 1)):
        base = (cluster // HALF) * SUB + (cluster % HALF) * CELL
        cbase = (cluster // HALF) * SUB + HALF * CELL + (cluster % HALF) * 2
        edge[side, 0:CELL, :] = local[base : base + CELL, :]
        edge[side, CELL : CELL + 2, :] = local[cbase : cbase + 2, :]
        edge[side, CELL + 2 : NODE, :] = jnp.zeros((NODE - CELL - 2, 2 * LEAF), jnp.float32)
    edges = [
        remote(edge.at[0], halo.at[1], e_send.at[0], e_recv.at[1], below),
        remote(edge.at[1], halo.at[0], e_send.at[1], e_recv.at[0], above),
    ]
    for copy in edges:
        copy.start()
    sent += edges

    for copy in asks:
        copy.wait_recv()
    move = pltpu.make_async_copy(asked_v, asked, q_local)
    move.start()
    move.wait()

    def pick(chunk, target, request):
        def one(c, carry):
            cell, row = request(c)
            target[pl.ds(pl.multiple_of(c * CELL, CELL), CELL), :] = chunk[pl.ds(cell * CELL, CELL), :]
            for part in range(2):
                target[pl.ds(CAP * CELL + c * 2 + part, 1), :] = chunk[pl.ds(row + part, 1), :]
            return carry

        lax.fori_loop(0, CAP, one, 0)

    arriving = []

    def select(slot):
        chunk = chunks[slot]
        source_z = (z + n_z - slot) % n_z
        for k in range(1, n_y):
            pick(chunk, stage.at[k - 1, slot], lambda c: (asked[k - 1, 0, source_z * CAP + c], asked[k - 1, 1, source_z * CAP + c]))
            copy = remote(
                stage.at[k - 1, slot], recv.at[k * n_z + slot], y_send.at[k - 1, slot], y_recv.at[k - 1, slot], across[k]
            )
            copy.start()
            sent.append(copy)
            arriving.append(copy)
        pick(chunk, recv.at[slot], lambda c: (own_requests[0, y * n_z + source_z, c], own_requests[1, y * n_z + source_z, c]))

    select(0)
    for step in range(1, n_z // 2 + 1):
        for way, part in order:
            if step - 1 < hops[way, part]:
                ring(way, part, step - 1).wait_recv()
                forward(way, part, step)
        select(step)
        if step < n_z // 2:
            select(n_z - step)
    for copy in arriving + edges:
        copy.wait_recv()
    for copy in sent:
        copy.wait_send()


def fetch(samples, coords, requests, n_leaf):
    n_z = n_leaf // ROWS_Y
    rows = samples.shape[0]
    half, cell = requests // HALF, requests % HALF
    places = jnp.stack([half * (SUB // CELL) + cell, half * SUB + HALF * CELL + cell * 2])
    sent_requests = jnp.swapaxes(places.reshape(2, ROWS_Y, n_z * CAP), 0, 1)
    sent_requests = jnp.pad(sent_requests, ((0, 0), (0, 6), (0, 0)))
    dma = pltpu.SemaphoreType.DMA
    f32 = jnp.float32
    return pl.pallas_call(
        functools.partial(fetch_body, n_leaf),
        out_shape=(
            jax.ShapeDtypeStruct((n_leaf, MSG, 2 * LEAF), f32),
            jax.ShapeDtypeStruct((2 * SUB, 2 * LEAF), f32),
            jax.ShapeDtypeStruct((2, NODE, 2 * LEAF), f32),
        ),
        in_specs=[whole, whole, scalars, whole],
        out_specs=(whole, whole, whole),
        scratch_shapes=[VMEM((2 * SUB, 2 * LEAF), f32)] * (n_z - 1)
        + [
            VMEM((ROWS_Y - 1, n_z, MSG, 2 * LEAF), f32),
            VMEM((2, NODE, 2 * LEAF), f32),
            VMEM((ROWS_Y - 1, 8, n_z * CAP), jnp.int32),
            pltpu.SMEM((ROWS_Y - 1, 8, n_z * CAP), jnp.int32),
            dma((2, 2, n_z // 2)),
            dma((2, 2, n_z // 2)),
            dma((ROWS_Y - 1, n_z)),
            dma((ROWS_Y - 1, n_z)),
            dma((ROWS_Y - 1,)),
            dma((ROWS_Y - 1,)),
            dma,
            dma((2,)),
            dma((2,)),
        ],
        compiler_params=pltpu.CompilerParams(
            collective_id=1, has_side_effects=True, vmem_limit_bytes=40 * MIB
        ),
        name="fetch",
    )(samples, coords, places, sent_requests)


def sample_body(
    leaves, recv, local, halo, target, slots, counts, near, sketch, far_out, near_out, partial_out, cells
):
    low16 = lanes((CELL, 2 * LEAF)) < LEAF
    low1 = lanes((1, 2 * LEAF)) < LEAF
    low32 = lanes((2 * CELL, 2 * LEAF)) < LEAF
    for c in range(leaves):
        base = (c // HALF) * SUB + (c % HALF) * CELL
        cbase = (c // HALF) * SUB + HALF * CELL + (c % HALF) * 2
        cells[c + 1, 0:CELL, :] = local[base : base + CELL, :]
        cells[c + 1, CELL : CELL + 2, :] = local[cbase : cbase + 2, :]
    cells[0] = halo[0]
    cells[leaves + 1] = halo[1]

    def halves(value):
        high = value.astype(jnp.bfloat16)
        return high, (value - high.astype(jnp.float32)).astype(jnp.bfloat16)

    def pair(coordinates, first, second):
        (block_a, row_a, last_a, scale_a), (block_b, row_b, last_b, scale_b) = first, second
        x = jnp.where(low1, row_a, swap_halves(row_b))
        yy = jnp.where(low1, swap_halves(row_a), row_b)
        zz = jnp.where(low1, last_a, last_b)
        dx = coordinates[0] - x
        dy = coordinates[1] - yy
        dz = coordinates[2] - zz
        values = jnp.exp(jnp.sqrt(dx * dx + dy * dy + dz * dz) * (-1.0 / length_scale))
        block_a = block_a * scale_a
        block_b = block_b * scale_b
        rows = jnp.concatenate(
            [jnp.where(low16, block_a, swap_halves(block_b)), jnp.where(low16, swap_halves(block_a), block_b)], axis=0
        )
        return halves(values), halves(rows)

    def four(coordinates, entries):
        (k0h, k0l), (s0h, s0l) = pair(coordinates, entries[0], entries[1])
        (k1h, k1l), (s1h, s1l) = pair(coordinates, entries[2], entries[3])
        left = jnp.concatenate(
            [jnp.concatenate([s0h, s1h], axis=1), jnp.concatenate([s0l, s1l], axis=1)], axis=0
        )
        right = jnp.concatenate(
            [jnp.concatenate([k0h, k1h], axis=1), jnp.concatenate([k0l, k1l], axis=1)], axis=0
        )
        return dot_nt(left, right, None)

    def far_entry(leaf, f, count):
        slot = slots[leaf, f]
        message = slot // CAP
        c = slot - message * CAP
        scale = jnp.where(f < count, 1.0, 0.0).astype(jnp.float32)
        return (
            recv[message, pl.ds(pl.multiple_of(c * CELL, CELL), CELL), :],
            recv[message, pl.ds(CAP * CELL + 2 * c, 1), :],
            recv[message, pl.ds(CAP * CELL + 2 * c + 1, 1), :],
            scale,
        )

    def near_entry(leaf, offset):
        at = leaf + offset
        scale = near[leaf * NEAR + offset].astype(jnp.float32) if offset < NEAR else jnp.float32(0)
        at = at if offset < NEAR else leaf
        return cells[at, 0:CELL, :], cells[at, CELL : CELL + 1, :], cells[at, CELL + 1 : CELL + 2, :], scale

    def fold(total):
        total = total[: 2 * CELL] + total[2 * CELL :]
        return total + swap_halves(total)

    def one_leaf(leaf):
        block = target[pl.ds(pl.multiple_of(leaf * LEAF, LEAF), LEAF), :]
        coordinates = [jnp.broadcast_to(block[:, a : a + 1], (LEAF, 2 * LEAF)) for a in range(3)]
        count = counts[leaf]

        def step(g, total):
            return total + four(coordinates, [far_entry(leaf, 4 * g + b, count) for b in range(4)])

        far = lax.fori_loop(0, (count + 3) // 4, step, jnp.zeros((2 * LEAF // 2, 2 * LEAF), jnp.float32))
        close = four(coordinates, [near_entry(leaf, o) for o in range(4)])
        return fold(far), fold(close)

    def two_leaves(j, carry):
        far_a, near_a = one_leaf(2 * j)
        far_b, near_b = one_leaf(2 * j + 1)
        far = jnp.where(low32, far_a, far_b)
        at = pl.ds(pl.multiple_of(j * 2 * LEAF, 2 * LEAF), 2 * LEAF)
        far_out[:, at] = far
        near_out[:, at] = jnp.where(low32, near_a, near_b)
        partial_out[:, at] = dot_nn(sketch[...], far)
        return carry

    lax.fori_loop(0, leaves // 2, two_leaves, 0)


def sample(recv, local, halo, target, slots, counts, near, sketch):
    leaves = counts.shape[0]
    shape = jax.ShapeDtypeStruct((RANK, leaves * LEAF), jnp.float32)
    return pl.pallas_call(
        functools.partial(sample_body, leaves),
        out_shape=(shape, shape, shape),
        in_specs=[whole, whole, whole, whole, scalars, scalars, scalars, whole],
        out_specs=(whole, whole, whole),
        scratch_shapes=[VMEM((leaves + 2, NODE, 2 * LEAF), jnp.float32)],
        compiler_params=pltpu.CompilerParams(vmem_limit_bytes=40 * MIB),
        name="sample",
    )(recv, local, halo, target, slots, counts, near, sketch)


def total_body(n, partial, out, parts, send_a, recv_a, send_b, recv_b):
    me = lax.axis_index("cols")
    width = partial.shape[1] // n
    peers = [(me + k) % n for k in range(1, n)]
    greet("cols", peers)

    def piece(owner):
        return pl.ds(pl.multiple_of(owner * width, width), width)

    first = []
    for k in range(1, n):
        copy = pltpu.make_async_remote_copy(
            src_ref=partial.at[:, piece(peers[k - 1])], dst_ref=parts.at[k - 1], send_sem=send_a.at[k - 1],
            recv_sem=recv_a.at[k - 1], device_id={"cols": peers[k - 1]}, device_id_type=MESH,
        )
        copy.start()
        first.append(copy)
    value = partial[:, piece(me)]
    for k in range(1, n):
        first[k - 1].wait_recv()
        value = value + parts[k - 1]
    out[:, piece(me)] = value
    second = []
    for k in range(1, n):
        copy = pltpu.make_async_remote_copy(
            src_ref=out.at[:, piece(me)], dst_ref=out.at[:, piece(me)], send_sem=send_b.at[k - 1],
            recv_sem=recv_b.at[k - 1], device_id={"cols": peers[k - 1]}, device_id_type=MESH,
        )
        copy.start()
        second.append(copy)
    for k in range(1, n):
        owner = (me + n - k) % n
        pltpu.make_async_remote_copy(
            src_ref=out.at[:, piece(owner)], dst_ref=out.at[:, piece(owner)], send_sem=send_b.at[k - 1],
            recv_sem=recv_b.at[k - 1], device_id={"cols": peers[k - 1]}, device_id_type=MESH,
        ).wait_recv()
    for copy in first + second:
        copy.wait_send()


def total(partial, n):
    rows, columns = partial.shape
    dma = pltpu.SemaphoreType.DMA
    return pl.pallas_call(
        functools.partial(total_body, n),
        out_shape=jax.ShapeDtypeStruct(partial.shape, jnp.float32),
        in_specs=[whole],
        out_specs=whole,
        scratch_shapes=[VMEM((n - 1, rows, columns // n), jnp.float32)] + [dma((n - 1,))] * 4,
        compiler_params=pltpu.CompilerParams(collective_id=2, has_side_effects=True),
        name="total",
    )(partial)


def eye(shape, first=0):
    rows = lax.broadcasted_iota(jnp.int32, shape, 0)
    return jnp.where(lanes(shape) == rows + first, 1.0, 0.0).astype(jnp.float32)


def compress(sketched_t):
    unit = eye((2 * RANK, 2 * RANK))
    shape = (RANK, 4 * RANK)
    on_diagonal = lanes(shape) == lax.broadcasted_iota(jnp.int32, shape, 0)
    tiles = []
    for b in sketched_t:
        tile = dot_nt(b, jnp.concatenate([b, b, unit], axis=0))
        diagonal = jnp.where(on_diagonal, tile, 0.0)
        trace = jnp.sum(jnp.sum(diagonal, axis=1, keepdims=True), axis=0, keepdims=True)
        tile = tile + jnp.where(on_diagonal, shift_share * trace / RANK + 1e-06, 0.0)
        tiles.append([tile[8 * g : 8 * g + 8] for g in range(4)])
    sub = lax.broadcasted_iota(jnp.int32, (8, 4 * RANK), 0)
    for k in range(RANK):
        g, s = k // 8, k % 8
        for tile in tiles:
            row = tile[g][s : s + 1, :]
            scaled = row * (1.0 / row[:, k : k + 1])
            for h in range(g, 4):
                column = tile[h][:, k : k + 1]
                if h == g:
                    if s == 7:
                        continue
                    tile[h] = tile[h] - jnp.where(sub > s, column, 0.0) * scaled
                else:
                    tile[h] = tile[h] - column * scaled
    done = []
    for tile in tiles:
        tile = jnp.concatenate(tile, axis=0)
        diagonal = jnp.sum(jnp.where(on_diagonal, tile, 0.0), axis=1, keepdims=True)
        done.append(tile * lax.rsqrt(diagonal))
    return done


def level(read, write, count, group):
    def some(start):
        inputs = [read(start + b) for b in range(min(group, count))]
        tiles = compress([b for b, _ in inputs])
        for b, (tile, (_, stacked)) in enumerate(zip(tiles, inputs)):
            padded = jnp.concatenate([jnp.zeros((2 * RANK, stacked.shape[1]), jnp.float32), stacked], axis=0)
            write(start + b, tile, dot_nn(tile, padded))

    if count <= group:
        some(0)
    else:
        lax.fori_loop(0, count // group, lambda g, carry: (some(g * group), carry)[1], 0)


def branch_body(leaves, sketched, far, basis, branch, packed, nodes, projected):
    low = lanes((RANK, 2 * LEAF)) < LEAF
    group = 8

    def some(g, carry):
        bs, rows = [], []
        for j in range(group // 2):
            at = pl.ds(pl.multiple_of((g * (group // 2) + j) * 2 * LEAF, 2 * LEAF), 2 * LEAF)
            b, row = sketched[:, at], far[:, at]
            bs += [b[:, :LEAF], swap_halves(b)[:, :LEAF]]
            rows += [jnp.where(low, 0.0, swap_halves(row)), jnp.where(low, 0.0, row)]
        tiles = compress(bs)
        for b, (tile, row) in enumerate(zip(tiles, rows)):
            nodes[g * group + b] = tile
            projected[g * group + b] = dot_nt(tile, row)
        for j in range(group // 2):
            at = pl.ds(pl.multiple_of((g * (group // 2) + j) * 2 * LEAF, 2 * LEAF), 2 * LEAF)
            basis[:, at] = jnp.where(low, swap_halves(tiles[2 * j]), tiles[2 * j + 1])
        return carry

    lax.fori_loop(0, leaves // group, some, 0)

    middle = eye((RANK, 4 * RANK), RANK)

    def read(node):
        pair = nodes[pl.ds(2 * node, 2)].reshape(2 * RANK, 4 * RANK)
        return dot_nt(middle, pair), projected[pl.ds(2 * node, 2)].reshape(2 * RANK, RANK)

    def write(node, tile, value):
        nodes[node] = tile
        projected[node] = value

    count = leaves // 2
    while count >= 1:
        level(read, write, count, 8)
        count //= 2
    branch[...] = projected[0]
    quarter = lanes((8, 4 * RANK)) // RANK
    wide = dot_nn(projected[0], eye((RANK, 4 * RANK)))
    tile = nodes[0]
    for i, (source, shift) in enumerate(((tile, RANK), (wide, 0))):
        row = jnp.zeros((8, 4 * RANK), jnp.float32)
        for g in range(4):
            turned = pltpu.roll(source[8 * g : 8 * g + 8], (RANK * g - shift) % (4 * RANK), 1)
            row = jnp.where(quarter == g, turned, row)
        packed[8 * i : 8 * i + 8] = row


def branch(sketched, far):
    leaves = sketched.shape[1] // LEAF
    f32 = jnp.float32
    return pl.pallas_call(
        functools.partial(branch_body, leaves),
        out_shape=(
            jax.ShapeDtypeStruct(sketched.shape, f32),
            jax.ShapeDtypeStruct((RANK, RANK), f32),
            jax.ShapeDtypeStruct((CELL, 4 * RANK), f32),
        ),
        in_specs=[whole, whole],
        out_specs=(whole, whole, whole),
        scratch_shapes=[VMEM((leaves, RANK, 4 * RANK), f32), VMEM((leaves, RANK, RANK), f32)],
        compiler_params=pltpu.CompilerParams(vmem_limit_bytes=40 * MIB),
        name="branch",
    )(sketched, far)


def gather_body(n_leaf, packed, out, y_send, y_recv, ring_send, ring_recv, own_sem):
    n_y = ROWS_Y
    n_z = n_leaf // n_y
    me = lax.axis_index("leaf")
    y, z = me // n_z, me % n_z
    up = y * n_z + (z + 1) % n_z
    down = y * n_z + (z + n_z - 1) % n_z
    across = [((y + k) % n_y) * n_z + z for k in range(1, n_y)]
    greet("leaf", [up, down] + across)
    sent = []
    for k in range(1, n_y):
        copy = pltpu.make_async_remote_copy(
            src_ref=packed, dst_ref=out.at[z, y], send_sem=y_send.at[k - 1], recv_sem=y_recv.at[k - 1],
            device_id={"leaf": across[k - 1]}, device_id_type=MESH,
        )
        copy.start()
        sent.append(copy)
    own = pltpu.make_async_copy(packed, out.at[z, y], own_sem)
    own.start()
    own.wait()
    for k in range(1, n_y):
        other = (y + n_y - k) % n_y
        pltpu.make_async_remote_copy(
            src_ref=packed, dst_ref=out.at[z, other], send_sem=y_send.at[k - 1], recv_sem=y_recv.at[k - 1],
            device_id={"leaf": across[k - 1]}, device_id_type=MESH,
        ).wait_recv()

    def hop(way, step, slot):
        return pltpu.make_async_remote_copy(
            src_ref=out.at[slot], dst_ref=out.at[slot], send_sem=ring_send.at[way, step],
            recv_sem=ring_recv.at[way, step], device_id={"leaf": up if way == 0 else down}, device_id_type=MESH,
        )

    hops = (n_z // 2, n_z // 2 - 1)
    for step in range(n_z // 2 + 1):
        for way in range(2):
            slot = (z + n_z - step) % n_z if way == 0 else (z + step) % n_z
            if 1 <= step <= hops[way]:
                hop(way, step - 1, slot).wait_recv()
            if step < hops[way]:
                copy = hop(way, step, slot)
                copy.start()
                sent.append(copy)
    for copy in sent:
        copy.wait_send()


def gather(packed, n_leaf):
    n_z = n_leaf // ROWS_Y
    dma = pltpu.SemaphoreType.DMA
    return pl.pallas_call(
        functools.partial(gather_body, n_leaf),
        out_shape=jax.ShapeDtypeStruct((n_z, ROWS_Y) + packed.shape, jnp.float32),
        in_specs=[whole],
        out_specs=whole,
        scratch_shapes=[
            dma((ROWS_Y - 1,)), dma((ROWS_Y - 1,)), dma((2, n_z // 2)), dma((2, n_z // 2)), dma,
        ],
        compiler_params=pltpu.CompilerParams(collective_id=3, has_side_effects=True),
        name="gather",
    )(packed)


def top_body(n_leaf, gathered, transfers, root, nodes, projected):
    n_z = n_leaf // ROWS_Y
    quarters = [eye((RANK, 4 * RANK), 0)]
    right = eye((2 * RANK, 4 * RANK), 2 * RANK)
    count = n_leaf // 2

    def unpack(block):
        return jnp.concatenate([pltpu.roll(block, (4 * RANK - RANK * g) % (4 * RANK), 1) for g in range(4)], axis=0)

    def read_first(node):
        pairs = []
        for part in range(2):
            a = gathered[(2 * node) % n_z, (2 * node) // n_z, 8 * part : 8 * part + 8, :]
            b = gathered[(2 * node + 1) % n_z, (2 * node + 1) // n_z, 8 * part : 8 * part + 8, :]
            pairs.append(jnp.concatenate([unpack(a), unpack(b)], axis=0))
        return dot_nt(quarters[0], pairs[0]), pairs[1]

    middle = eye((RANK, 4 * RANK), RANK)

    def read(node):
        pair = nodes[pl.ds(2 * node, 2)].reshape(2 * RANK, 4 * RANK)
        return dot_nt(middle, pair), projected[pl.ds(2 * node, 2)].reshape(2 * RANK, 4 * RANK)

    first = 0
    reader = read_first
    while count >= 1:

        def write(node, tile, value, first=first):
            nodes[node] = tile
            projected[node] = value
            transfers[first + node] = dot_nt(right, tile)

        level(reader, write, count, 8)
        reader = read
        first += count
        count //= 2
    root[...] = projected[0][:, :RANK]


def top(gathered, n_leaf):
    f32 = jnp.float32
    return pl.pallas_call(
        functools.partial(top_body, n_leaf),
        out_shape=(
            jax.ShapeDtypeStruct((n_leaf - 1, 2 * RANK, RANK), f32),
            jax.ShapeDtypeStruct((RANK, RANK), f32),
        ),
        in_specs=[whole],
        out_specs=(whole, whole),
        scratch_shapes=[VMEM((n_leaf // 2, RANK, 4 * RANK), f32), VMEM((n_leaf // 2, RANK, 4 * RANK), f32)],
        compiler_params=pltpu.CompilerParams(vmem_limit_bytes=40 * MIB),
        name="top",
    )(gathered)


def on_device(n_leaf, n_cols, points, samples, sketch, far_requests, far_slots, far_count, near_mask):
    n_z = n_leaf // ROWS_Y
    leaves = far_count.shape[0]
    me = lax.axis_index("leaf")
    y, z = me // n_z, me % n_z
    coords = points.reshape(3, leaves, LEAF)
    packed_coords = jnp.stack(
        [jnp.concatenate([coords[0], coords[1]], axis=1), jnp.concatenate([coords[2], coords[2]], axis=1)], axis=1
    ).reshape(2 * leaves, 2 * LEAF)
    target = jnp.pad(points.T, ((0, 0), (0, 5)))
    owner = far_slots // CAP
    slots = (((y - owner // n_z) % ROWS_Y) * n_z + (z - owner % n_z) % n_z) * CAP + far_slots % CAP
    places = me * leaves + jnp.arange(leaves)[:, None] + jnp.arange(NEAR)[None, :] - NEAR // 2
    inside = (places >= 0) & (places < n_leaf * leaves)
    near = jnp.where(inside, near_mask, 0).reshape(-1)

    recv, local, halo = fetch(samples, packed_coords, far_requests[0], n_leaf)
    far_sample, near_sample, partial = sample(recv, local, halo, target, slots, far_count, near, sketch)
    sketched = total(partial, n_cols)
    leaf_basis, branch_samples, packed = branch(sketched, far_sample)
    gathered = gather(packed, n_leaf)
    top_transfer, root_sample = top(gathered, n_leaf)
    return far_sample, near_sample, leaf_basis, branch_samples, top_transfer, root_sample


def solution(mesh):
    return jax.shard_map(
        functools.partial(on_device, mesh.shape["leaf"], mesh.shape["cols"]),
        mesh=mesh,
        in_specs=(
            P(None, "leaf"),
            P("cols", "leaf"),
            P(None, "cols"),
            P("leaf", None, None),
            P("leaf", None),
            P("leaf"),
            P("leaf", None),
        ),
        out_specs=(
            P("cols", "leaf"),
            P("cols", "leaf"),
            P(None, "leaf"),
            P("leaf", "cols"),
            P(),
            P(None, "cols"),
        ),
        check_vma=False,
    )
```

time: 1460 us -> 264 us (0.18)
  the two profiles are of different devices: /device:TPU:8 before, /device:TPU:64 now
where the time goes in v1:
time: 264 us; the launch traced here: 263 us
  Pallas kernels  249 us (94%)
  local copies, waits for them, and re-layouts  11.8 us (4%)
    pallas_call x1, Pallas kernels, fetch(): pl.pallas_call(functools.partial(fetch_body, n_leaf), out_shape=(jax.Shap...  69.1 us
    pallas_call x1, Pallas kernels, top(): pl.pallas_call(functools.partial(top_body, n_leaf), out_shape=(jax.ShapeD...  49.2 us
    pallas_call x1, Pallas kernels, branch(): pl.pallas_call(functools.partial(branch_body, leaves), out_shape=(jax.Sha...  42.8 us
    pallas_call x1, Pallas kernels, gather(): pl.pallas_call(functools.partial(gather_body, n_leaf), out_shape=jax.Shap...  35.9 us
    pallas_call x1, Pallas kernels, sample(): pl.pallas_call(functools.partial(sample_body, leaves), out_shape=(shape,...  35.7 us
    pallas_call x1, Pallas kernels, total(): pl.pallas_call(functools.partial(total_body, n), out_shape=jax.ShapeDtype...  16.1 us
    unnamed x19, local copies, waits for them, and re-layouts  9.99 us

profile of v1, /device:TPU:64, one launch (start us, length us, event | category | flops | bytes accessed | tf_op | source)
XLA Modules:
  0.0 263.1 jit_solution(2238957101400969661)
XLA Ops:
  0.7 0.7 fusion.15
  1.4 0.7 multiply_add_fusion.1
  2.1 0.1 copy.47
  2.2 0.1 reshape.34.near
  2.3 0.8 copy.43
  3.1 0.9 slice_reduce_fusion.2
  4.5 0.1 stack.24
  4.7 0.1 stack.25
  4.9 1.1 copy.42
  6.1 0.9 copy-done.2
  7.1 69.1 %fetch.1 = (f32[64,144,128]{2,1,0:T(8,128)S(1)}, f32[576,128]{1,0:T(8,128)S(1)}, f32[2,24,128]{2,1,0:T(8,128)S(1)}) custom-call(f32[32,2048]{1,0:T(8,128)S(1)} %copy-done.2, f32[64,128]{1,0:T(8,128)S(1)} %bitcast.8, s32[2,64,8]{2,1,0:T(8,128)S(1)} %copy.41.own_requests, s32[4,8,128]{2,1,0:T(8,128)S(1)} %pad.8.sent_requests), custom_call_target="tpu_custom_call" | custom-call | tf_op jit(solution)/shard_map/fetch/pallas_call | solution.py:189
  76.2 0.7 copy-done.5
  77.0 0.7 copy-done.7
  77.6 35.7 %sample.1 = (f32[32,2048]{1,0:T(8,128)}, f32[32,2048]{1,0:T(8,128)}, f32[32,2048]{1,0:T(8,128)S(1)}) custom-call(f32[64,144,128]{2,1,0:T(8,128)S(1)} %get-tuple-element.17.recv, f32[576,128]{1,0:T(8,128)S(1)} %get-tuple-element.18.local, f32[2,24,128]{2,1,0:T(8,128)S(1)} %get-tuple-element.19.halo, f32[2048,8]{1,0:T(8,128)S(1)} %pad.9.target, ...), custom_call_target="tpu_custom_call" | custom-call | tf_op jit(solution)/shard_map/sample/pallas_call | solution.py:316
  113.4 0.7 copy-done.4
  114.1 16.1 %total.1.sketched = f32[32,2048]{1,0:T(8,128)} custom-call(f32[32,2048]{1,0:T(8,128)} %copy-done.4), custom_call_target="tpu_custom_call" | custom-call | tf_op jit(solution)/shard_map/total/pallas_call | solution.py:370
  130.2 0.9 copy-done.1
  131.1 0.9 copy-done.3
  132.1 42.8 %branch.1 = (f32[32,2048]{1,0:T(8,128)}, f32[32,32]{1,0:T(8,128)}, f32[16,128]{1,0:T(8,128)S(1)}) custom-call(f32[32,2048]{1,0:T(8,128)S(1)} %copy-done.1, f32[32,2048]{1,0:T(8,128)S(1)} %copy-done.3), custom_call_target="tpu_custom_call" | custom-call | tf_op jit(solution)/shard_map/branch/pallas_call | solution.py:484
  174.8 0.6 copy-done.6
  175.4 35.9 %gather.1.gathered = f32[16,4,16,128]{3,2,1,0:T(8,128)} custom-call(f32[16,128]{1,0:T(8,128)} %copy-done.6), custom_call_target="tpu_custom_call" | custom-call | tf_op jit(solution)/shard_map/gather/pallas_call | solution.py:549
  211.3 1.0 copy-done
  212.4 49.2 %top.1 = (f32[63,64,32]{2,1,0:T(8,128)S(1)}, f32[32,32]{1,0:T(8,128)}) custom-call(f32[16,4,16,128]{3,2,1,0:T(8,128)S(1)} %copy-done), custom_call_target="tpu_custom_call" | custom-call | tf_op jit(solution)/shard_map/top/pallas_call | solution.py:603
  261.6 1.6 copy.48
  (23 shorter events, 0.8 us)
Async XLA Ops:
  6.1 1.0 copy-start.2
  76.2 0.7 copy-start.5
  77.0 0.7 copy-start.7
  113.4 0.7 copy-start.4
  130.2 1.0 copy-start.1
  131.1 0.9 copy-start.3
  174.8 0.6 copy-start.6
  211.3 1.0 copy-start
